TPU v7x, 256 devices: a whole 4x4x8 slice. The times are simulated.
256 devices in a mesh: dp: 8 (over z), graph: 32 (over x, y, core).
Axes of the slice: x: 4, y: 4, z: 8, core: 2. Of those that a mesh axis runs over, the one named last changes fastest.
Arguments:
- node_feats: bfloat16 [8, 224, 49, 256], P('dp', 'graph'), may hold values from -0.125 to 0.125
- node_grads: bfloat16 [8, 224, 49, 256], P('dp', 'graph'), may hold values from -1.75 to 1.75
- node_row: int32 [8, 224], P('dp'), may hold values from 0 to 223, as said below
- edge_src: int32 [8, 16384], P('dp', 'graph'), may hold values from 0 to 223, as said below
- edge_tgt: int32 [8, 16384], P('dp', 'graph'), may hold values from 0 to 223, as said below
- edge_rot: int32 [8, 16384], P('dp', 'graph'), may hold values from 0 to 2047
- edge_len: float32 [8, 16384], P('dp', 'graph'), may hold values from 0.5 to 11.5
- edge_count: int32 [8, 32], P('dp', 'graph'), may hold values from 64 to 512, as said below
- rotations: bfloat16 [2048, 7, 49], replicated, as said below
- w_zero: bfloat16 [1792, 1792], replicated, may hold values from -0.125 to 0.125
- w_radial: float32 [600, 256], replicated, may hold values from -3 to 3
Outputs:
- node_grad: float32 [8, 224, 49, 256], P('dp', 'graph')
- weight_grad: float32 [1792, 1792], P('graph')
Inputs may be any that keep to these rules, and one draw needn't show every extreme that they name: Each row of node_row is a permutation: atom i of a batch graph is held at row node_row[b, i], and graph index g holds rows g * 7 to (g + 1) * 7 - 1. `edge_tgt`: for every slot of the block of graph index g, the target atom is held at one of the rows g * 7 to (g + 1) * 7 - 1. `edge_src`: among the 512 slots of the block of one index of graph, at most 24 have source atoms held by the same index of graph; in every batch graph one index of graph holds the source atoms of exactly 24 live slots of every block. The first edge_count[b, g] slots of a block are live, the others are padding with valid ids; in every batch graph one index of graph has all 512 slots live. `rotations`: row l of each rotation is zero outside the coefficients of degree l (coefficients l * l to l * l + 2 l).
All inputs are finite; a program needn't handle non-finite values.
Results may differ from a plain program's by a relative error of at most 0.0041.
Values may be sent and summed in bfloat16 or wider, within the bound.
A program may use at most 256 MiB of HBM per device.

v0:
```python
import jax
import jax.numpy as jnp
from jax import lax
from jax.sharding import PartitionSpec as P

BLOCK = 256
CUTOFF = 12.0


def radial_profile(lengths, w_radial):
    gauss_count = w_radial.shape[0]
    spacing = CUTOFF / (gauss_count - 1)
    centers = jnp.arange(gauss_count).astype(jnp.float32) * spacing
    basis = jnp.exp(-0.5 / (2.0 * spacing) ** 2 * (lengths[:, None] - centers[None, :]) ** 2)
    return jnp.dot(
        basis, w_radial, precision=lax.Precision.HIGHEST, preferred_element_type=jnp.float32
    )


def find_rows(atom_ids, row_table):
    matches = atom_ids[:, None] == jnp.arange(row_table.shape[0], dtype=jnp.int32)[None, :]
    return jnp.sum(jnp.where(matches, row_table[None, :], 0), axis=1)


def forward_rows(turning, source, radial):
    rotated = jnp.einsum("bij,bjc->bic", turning, source, preferred_element_type=jnp.float32)
    return (rotated * radial[:, None, :]).astype(jnp.bfloat16)


def backward_terms(edge_in, target, turning, radial, w_zero):
    edge_grad = jnp.einsum(
        "bij,bjc->bic", turning, target, preferred_element_type=jnp.float32
    ).astype(jnp.bfloat16)
    edge_rows = edge_in.shape[0]
    flat_in = edge_in.reshape(edge_rows, -1)
    flat_grad = edge_grad.reshape(edge_rows, -1)
    weight_term = lax.dot_general(
        flat_in, flat_grad, (((0,), (0,)), ((), ())), preferred_element_type=jnp.float32
    )
    hidden = lax.dot_general(
        flat_grad, w_zero, (((1,), (1,)), ((), ())), preferred_element_type=jnp.float32
    )
    returned = (hidden.reshape(edge_in.shape) * radial[:, None, :]).astype(jnp.bfloat16)
    return (weight_term, returned)


def spread_back(turning, returned):
    return jnp.einsum("bij,bic->bjc", turning, returned, preferred_element_type=jnp.float32)


def per_device(
    node_feats,
    node_grads,
    node_row,
    edge_src,
    edge_tgt,
    edge_rot,
    edge_len,
    edge_count,
    rotations,
    w_zero,
    w_radial,
):
    node_dev = node_feats.shape[1]
    own_index = lax.axis_index("graph")
    row_table = node_row[0]
    grad_table = node_grads[0]
    source_ids = edge_src[0]
    target_rows = find_rows(edge_tgt[0], row_table) - own_index * node_dev
    turn_ids = edge_rot[0]
    lengths = edge_len[0]
    live_count = edge_count[0, 0]
    source_rows = find_rows(source_ids, row_table)
    square = w_zero.shape[0]
    blocks = (live_count + BLOCK - 1) // BLOCK
    sources_all = lax.all_gather(node_feats, "graph", axis=1, tiled=True)[0]

    def advance(step_index, carry):
        weight_acc, node_acc = carry
        first = step_index * BLOCK
        here_source = lax.dynamic_slice_in_dim(source_rows, first, BLOCK)
        here_target = lax.dynamic_slice_in_dim(target_rows, first, BLOCK)
        here_turn = lax.dynamic_slice_in_dim(turn_ids, first, BLOCK)
        here_length = lax.dynamic_slice_in_dim(lengths, first, BLOCK)
        alive_mask = (first + jnp.arange(BLOCK, dtype=jnp.int32) < live_count).astype(jnp.float32)
        radial = radial_profile(here_length, w_radial) * alive_mask[:, None]
        turning = rotations[here_turn]
        edge_in = forward_rows(turning, sources_all[here_source], radial)
        weight_term, returned = backward_terms(
            edge_in, grad_table[here_target], turning, radial, w_zero
        )
        return (
            weight_acc + weight_term,
            node_acc.at[here_source].add(spread_back(turning, returned)),
        )

    start_state = (
        jnp.zeros((square, square), jnp.float32),
        jnp.zeros(sources_all.shape, jnp.float32),
    )
    weight_acc, node_acc = lax.fori_loop(0, blocks, advance, start_state)
    node_part = lax.psum_scatter(node_acc[None], "graph", scatter_dimension=1, tiled=True)
    rows_part = lax.psum_scatter(weight_acc, "graph", scatter_dimension=0, tiled=True)
    weight_grad = lax.psum(rows_part, "dp")
    return (node_part, weight_grad)


def solution(mesh):
    placed = (
        P("dp", "graph", None, None),
        P("dp", "graph", None, None),
        P("dp", None),
        P("dp", "graph"),
        P("dp", "graph"),
        P("dp", "graph"),
        P("dp", "graph"),
        P("dp", "graph"),
        P(),
        P(),
        P(),
    )
    return jax.shard_map(
        per_device,
        mesh=mesh,
        in_specs=placed,
        out_specs=(P("dp", "graph", None, None), P("graph", None)),
        check_vma=False,
    )
```

profile of v0, /device:TPU:2, one launch (start us, length us, event | category | flops | bytes accessed | tf_op | source)
XLA Modules:
  0.0 616.0 jit_solution(6712216942642518904)
XLA Ops:
  7.2 0.7 all-gather.2.cloned.1.call-update
  8.6 5.6 copy.34
  14.2 0.9 select_reduce_fusion
  15.1 52.0 %all-gather.2.cloned.1.call-done = bf16[1,224,49,256]{3,2,0,1:T(8,128)(2,1)} async-done(((bf16[1,7,49,256]{3,2,0,1:T(8,128)(2,1)}), bf16[1,224,49,256]{3,2,0,1:T(8,128)(2,1)}) %all-gather.2.cloned.1.call-update) | async-done | bytes 5619728 | tf_op jit(solution)/shard_map/all_gather | solution.py:76
  67.1 5.5 broadcast_in_dim.44
  72.6 5.4 broadcast_in_dim.45
  78.1 100.3 %while.12 = (s32[]{:T(128)}, f32[1792,1792]{1,0:T(8,128)}, f32[224,49,256]{2,1,0:T(8,128)}, s32[]{:T(128)}, s32[512]{0:T(512)S(1)}, /*index=5*/bf16[2048,7,49]{2...) while((s32[]{:T(128)}, f32[1792,1792]{1,0:T(8,128)}, ...), condition=%wide.region_4.5_spmd, body=%wide.region_2.4_spmd.sunk | while | flops 3904316672 | bytes 142397968 | solution.py:101
  78.3 0.1 compare_select_fusion.5
  78.4 3.0 gather_fusion
  81.4 0.1 compare_select_fusion.6
  81.5 6.8 %gather_fusion.1 = bf16[256,49,256]{2,1,0:T(8,128)(2,1)} fusion(bf16[224,49,256]{2,1,0:T(8,128)(2,1)} %get-tuple-element.287, s32[1024]{0:T(1024)S(1)} %pad_clamp_fusion.7), kind=kCustom, calls=%fused_computation.1.clone.1 | custom fusion | bytes 12846080 | tf_op jit(solution)/shard_map/while/body/gather | solution.py:88
  88.3 0.1 dynamic_slice.20
  88.4 0.6 compare_convert_fusion.2
  89.0 0.9 convolution_multiply_fusion.2
  89.9 4.4 multiply_convert_fusion.2
  94.4 0.8 copy.49
  95.2 4.0 gather_fusion.2
  99.2 4.4 convolution_convert_fusion.2
  103.6 1.6 copy.50
  105.1 11.9 %convolution_add_fusion.2 = f32[1792,1792]{1,0:T(8,128)} fusion(f32[1792,1792]{1,0:T(8,128)} %get-tuple-element.263, bf16[256,1792]{0,1:T(8,128)(2,1)S(1)} %bitcast.58, bf16[256,1792]{0,1:T(8,128)(2,1)} %bitcast.59), kind=kOutput, calls=%fused_computation.4.clone.1 | convolution fusion | flops 1647378432 | bytes 27525120 | tf_op jit(solution)/shard_map/while/body/dot_general | solution.py:37
  117.0 4.7 fusion.49
  121.7 7.3 %fusion.50 = f32[256,49,256]{2,1,0:T(8,128)} fusion(bf16[256,7,49]{2,1,0:T(8,128)(2,1)S(1)} %gather_fusion, f32[256,7,256]{2,0,1:T(8,128)S(1)} %fusion.49, f32[256,256]{1,0:T(8,128)S(1)} %convolution_multiply_fusion.2), kind=kOutput, calls=%fused_computation.10.clone.1 | convolution fusion | flops 45875200 | bytes 15117824 | tf_op jit(solution)/shard_map/while/body/bij,bic->bjc/dot_general | solution.py:48
  129.1 49.3 %scatter_fusion = f32[224,49,256]{2,1,0:T(8,128)} fusion(f32[224,49,256]{2,1,0:T(8,128)} %get-tuple-element.264, s32[256]{0:T(256)S(1)} %get-tuple-element.242, f32[256,49,256]{2,1,0:T(8,128)} %fusion.50), kind=kCustom, calls=%fused_computation.3.clone.1 | custom fusion | flops 3211264 | bytes 38536192 | tf_op jit(solution)/shard_map/while/body/scatter-add | solution.py:94
  178.3 0.0 all-reduce.6.cloned.1.call-start
  178.4 14.6 %copy.36 = f32[1,224,49,256]{3,0,2,1:T(1,128)} copy(f32[1,224,49,256]{3,2,1,0:T(8,128)} %bitcast.56) | data formatting | bytes 22478848 | tf_op jit(solution)/shard_map/broadcast_in_dim | solution.py:102
  193.0 0.0 all-reduce.4.cloned.1.call-start
  193.1 197.9 %reduce-scatter.2.cloned.1.call-done = f32[56,1792]{1,0:T(8,128)} async-done(((f32[1792,1792]{1,0:T(8,128)}), f32[56,1792]{1,0:T(8,128)}) %reduce-scatter.2.cloned.1.call-update) | async-done | bytes 401424 | tf_op jit(solution)/shard_map/reduce_scatter | solution.py:103
  391.0 0.6 dynamic-slice
  392.2 140.3 %all-reduce.6.cloned.1.call-done = f32[1,224,49,256]{3,0,2,1:T(1,128)} async-done(((f32[1,224,49,256]{3,0,2,1:T(1,128)}), f32[1,224,49,256]{3,0,2,1:T(1,128)}) %all-reduce.6.cloned.1.call-update) | async-done | bytes 11239440
  532.5 2.0 constant_dynamic-slice_fusion
  534.4 73.3 %all-reduce.4.cloned.1.call-done = f32[56,1792]{1,0:T(8,128)} async-done(((f32[56,1792]{1,0:T(8,128)}), f32[56,1792]{1,0:T(8,128)}) %all-reduce.4.cloned.1.call-update) | async-done | bytes 401424 | tf_op jit(solution)/shard_map/psum | solution.py:104
  607.7 1.8 copy.64
  (24 shorter events, 0.2 us)
Async XLA Ops:
  7.2 59.9 %all-gather.2.cloned.1.call-start = ((), (), s32[]{:S(2)}) async-start(), calls=%async_computation.1 | async-start | bytes 6623232 | tf_op jit(solution)/shard_map/all_gather | solution.py:76
  7.9 383.0 %reduce-scatter.2.cloned.1.call-start = ((), (), s32[]{:S(2)}) async-start(), calls=%async_computation.2 | async-start | bytes 13246464 | tf_op jit(solution)/shard_map/reduce_scatter | solution.py:103
  72.6 5.4 copy-start
  72.6 5.4 copy-start.2
  72.6 5.4 copy-start.3
  72.6 5.4 copy-start.4
  105.1 11.9 %copy-start.1 = (bf16[256,7,256]{0,2,1:T(8,128)(2,1)S(1)}, bf16[256,7,256]{0,2,1:T(8,128)(2,1)}, u32[]{:S(2)}) copy-start(bf16[256,7,256]{0,2,1:T(8,128)(2,1)} %copy.50) | copy-start | bytes 2752516 | tf_op jit(solution)/shard_map/while
  129.0 49.3 %copy-start.5 = (f32[600,256]{1,0:T(8,128)S(1)}, f32[600,256]{1,0:T(8,128)}, u32[]{:S(2)}) copy-start(f32[600,256]{1,0:T(8,128)} %get-tuple-element.334) | copy-start | bytes 1843204 | tf_op jit(solution)/shard_map/while
  178.3 354.2 %all-reduce.6.cloned.1.call-start = ((), (), s32[]{:S(2)}) async-start(), calls=%async_computation.4 | async-start | bytes 22478848
  193.0 198.0 %copy-start.6 = (u32[256]{0:T(256)S(1)}, u32[256]{0:T(256)}, u32[]{:S(2)}) copy-start(u32[256]{0:T(256)} %constant.58) | copy-start | bytes 3076
  193.0 414.7 %all-reduce.4.cloned.1.call-start = ((), (), s32[]{:S(2)}) async-start(), calls=%async_computation.3 | async-start | bytes 802816 | tf_op jit(solution)/shard_map/psum | solution.py:104
Sparse Core Ops, SparseCore 0:
  10.6 56.4 all-gather.1
  178.5 212.4 reduce-scatter.1
  394.4 137.9 all-reduce.5
  534.7 72.9 all-reduce.3
where the time goes:
time: 618 us; the launch traced here: 616 us
  waiting for transfers between devices  464 us (75%)
  local copies, waits for them, and re-layouts  51.7 us (8%)
  other arithmetic  51 us (8%)
  matrix products  33.7 us (5%)
  between operations  15.1 us (2%)
    reduce_scatter x1, waiting for transfers between devices, per_device(): lax.psum_scatter(weight_acc, 'graph', scatter_dimension=0, tiled=True)  198 us
    unnamed x5, waiting for transfers between devices  141 us
    psum x1, waiting for transfers between devices, per_device(): weight_grad = lax.psum(rows_part, 'dp')  73.3 us
    all_gather x1, waiting for transfers between devices, per_device(): sources_all = lax.all_gather(node_feats, 'graph', axis=1, tiled=True)[0]  52 us
    scatter-add x1, other arithmetic, advance(): node_acc.at[here_source].add(spread_back(turning, returned))  49.3 us
    broadcast_in_dim x1, local copies, waits for them, and re-layouts, per_device(): node_acc[None]  14.6 us
  transfers between devices with their start and end apart: 4, of which 4 were waited for; matrix products, arithmetic and copies ran while one was open for 4% of the time, Pallas kernels for 0%

commit v1 on v0

--- a/solution.py
+++ b/solution.py
@@ -101,7 +101,7 @@
     weight_acc, node_acc = lax.fori_loop(0, blocks, advance, start_state)
     node_part = lax.psum_scatter(node_acc[None], "graph", scatter_dimension=1, tiled=True)
     rows_part = lax.psum_scatter(weight_acc, "graph", scatter_dimension=0, tiled=True)
-    weight_grad = lax.psum(rows_part, "dp")
+    weight_grad = jnp.sum(lax.all_gather(rows_part, "dp"), axis=0)
     return (node_part, weight_grad)
 
 

time: 618 us -> 591 us (0.956)
  waiting for transfers between devices: 464 us -> 436 us
    psum x1 -> x0, waiting for transfers between devices: 73.3 us -> none  [per_device(): weight_grad = lax.psum(rows_part, 'dp')]
    all_gather x0 -> x1, waiting for transfers between devices: none -> 45.1 us  [per_device(): weight_grad = jnp.sum(lax.all_gather(rows_part, 'dp'), axis=0)]
where the time goes in v1:
time: 591 us; the launch traced here: 589 us
  waiting for transfers between devices  436 us (74%)
  other arithmetic  53.9 us (9%)
  local copies, waits for them, and re-layouts  49.9 us (8%)
  matrix products  33.7 us (6%)
  between operations  15.1 us (3%)
    reduce_scatter x1, waiting for transfers between devices, per_device(): lax.psum_scatter(weight_acc, 'graph', scatter_dimension=0, tiled=True)  198 us
    unnamed x5, waiting for transfers between devices  141 us
    all_gather x1, waiting for transfers between devices, per_device(): sources_all = lax.all_gather(node_feats, 'graph', axis=1, tiled=True)[0]  52 us
    scatter-add x1, other arithmetic, advance(): node_acc.at[here_source].add(spread_back(turning, returned))  49.3 us
    all_gather x1, waiting for transfers between devices, per_device(): weight_grad = jnp.sum(lax.all_gather(rows_part, 'dp'), axis=0)  45.1 us
    broadcast_in_dim x1, local copies, waits for them, and re-layouts, per_device(): node_acc[None]  14.6 us
    dot_general x1, matrix products, backward_terms(): lax.dot_general(flat_in, flat_grad, (((0,), (0,)), ((), ())), preferred_e...  11.9 us
  transfers between devices with their start and end apart: 4, of which 4 were waited for; matrix products, arithmetic and copies ran while one was open for 4% of the time, Pallas kernels for 0%

profile of v1, /device:TPU:2, one launch (start us, length us, event | category | flops | bytes accessed | tf_op | source)
XLA Modules:
  0.0 588.6 jit_solution(6387832146441671609)
XLA Ops:
  7.2 0.7 all-gather.4.cloned.1.call-update
  8.6 5.6 copy.34
  14.2 0.9 select_reduce_fusion
  15.1 52.0 %all-gather.4.cloned.1.call-done = bf16[1,224,49,256]{3,2,0,1:T(8,128)(2,1)} async-done(((bf16[1,7,49,256]{3,2,0,1:T(8,128)(2,1)}), bf16[1,224,49,256]{3,2,0,1:T(8,128)(2,1)}) %all-gather.4.cloned.1.call-update) | async-done | bytes 5619728 | tf_op jit(solution)/shard_map/all_gather | solution.py:76
  67.1 5.5 broadcast_in_dim.44
  72.6 5.4 broadcast_in_dim.45
  78.1 100.3 %while.12 = (s32[]{:T(128)}, f32[1792,1792]{1,0:T(8,128)}, f32[224,49,256]{2,1,0:T(8,128)}, s32[]{:T(128)}, s32[512]{0:T(512)S(1)}, /*index=5*/bf16[2048,7,49]{2...) while((s32[]{:T(128)}, f32[1792,1792]{1,0:T(8,128)}, ...), condition=%wide.region_4.5_spmd, body=%wide.region_2.4_spmd.sunk | while | flops 3904316672 | bytes 142397968 | solution.py:101
  78.3 0.1 compare_select_fusion.5
  78.4 3.0 gather_fusion
  81.4 0.1 compare_select_fusion.6
  81.5 6.8 %gather_fusion.1 = bf16[256,49,256]{2,1,0:T(8,128)(2,1)} fusion(bf16[224,49,256]{2,1,0:T(8,128)(2,1)} %get-tuple-element.287, s32[1024]{0:T(1024)S(1)} %pad_clamp_fusion.7), kind=kCustom, calls=%fused_computation.1.clone.1 | custom fusion | bytes 12846080 | tf_op jit(solution)/shard_map/while/body/gather | solution.py:88
  88.3 0.1 dynamic_slice.20
  88.4 0.6 compare_convert_fusion.2
  89.0 0.9 convolution_multiply_fusion.2
  89.9 4.4 multiply_convert_fusion.2
  94.4 0.8 copy.49
  95.2 4.0 gather_fusion.2
  99.2 4.4 convolution_convert_fusion.2
  103.6 1.6 copy.50
  105.1 11.9 %convolution_add_fusion.2 = f32[1792,1792]{1,0:T(8,128)} fusion(f32[1792,1792]{1,0:T(8,128)} %get-tuple-element.263, bf16[256,1792]{0,1:T(8,128)(2,1)S(1)} %bitcast.59, bf16[256,1792]{0,1:T(8,128)(2,1)} %bitcast.60), kind=kOutput, calls=%fused_computation.4.clone.1 | convolution fusion | flops 1647378432 | bytes 27525120 | tf_op jit(solution)/shard_map/while/body/dot_general | solution.py:37
  117.0 4.7 fusion.49
  121.7 7.3 %fusion.50 = f32[256,49,256]{2,1,0:T(8,128)} fusion(bf16[256,7,49]{2,1,0:T(8,128)(2,1)S(1)} %gather_fusion, f32[256,7,256]{2,0,1:T(8,128)S(1)} %fusion.49, f32[256,256]{1,0:T(8,128)S(1)} %convolution_multiply_fusion.2), kind=kOutput, calls=%fused_computation.10.clone.1 | convolution fusion | flops 45875200 | bytes 15117824 | tf_op jit(solution)/shard_map/while/body/bij,bic->bjc/dot_general | solution.py:48
  129.1 49.3 %scatter_fusion = f32[224,49,256]{2,1,0:T(8,128)} fusion(f32[224,49,256]{2,1,0:T(8,128)} %get-tuple-element.264, s32[256]{0:T(256)S(1)} %get-tuple-element.242, f32[256,49,256]{2,1,0:T(8,128)} %fusion.50), kind=kCustom, calls=%fused_computation.3.clone.1 | custom fusion | flops 3211264 | bytes 38536192 | tf_op jit(solution)/shard_map/while/body/scatter-add | solution.py:94
  178.3 0.0 all-reduce.3.cloned.1.call-start
  178.4 14.6 %copy.36 = f32[1,224,49,256]{3,0,2,1:T(1,128)} copy(f32[1,224,49,256]{3,2,1,0:T(8,128)} %bitcast.57) | data formatting | bytes 22478848 | tf_op jit(solution)/shard_map/broadcast_in_dim | solution.py:102
  193.0 0.0 all-gather.6.cloned.1.call-start
  193.1 197.9 %reduce-scatter.2.cloned.1.call-done = f32[56,1792]{1,0:T(8,128)} async-done(((f32[1792,1792]{1,0:T(8,128)}), f32[56,1792]{1,0:T(8,128)}) %reduce-scatter.2.cloned.1.call-update) | async-done | bytes 401424 | tf_op jit(solution)/shard_map/reduce_scatter | solution.py:103
  391.0 0.6 dynamic-slice
  392.2 140.0 %all-reduce.3.cloned.1.call-done = f32[1,224,49,256]{3,0,2,1:T(1,128)} async-done(((f32[1,224,49,256]{3,0,2,1:T(1,128)}), f32[1,224,49,256]{3,0,2,1:T(1,128)}) %all-reduce.3.cloned.1.call-update) | async-done | bytes 11239440
  532.2 2.0 constant_dynamic-slice_fusion
  534.2 45.1 %all-gather.6.cloned.1.call-done = f32[448,1792]{1,0:T(8,128)} async-done(((f32[56,1792]{1,0:T(8,128)}), f32[448,1792]{1,0:T(8,128)}) %all-gather.6.cloned.1.call-update) | async-done | bytes 3211280 | tf_op jit(solution)/shard_map/all_gather | solution.py:104
  579.3 2.9 reduce_sum.29
  (24 shorter events, 0.2 us)
Async XLA Ops:
  7.2 59.9 %all-gather.4.cloned.1.call-start = ((), (), s32[]{:S(2)}) async-start(), calls=%async_computation.1 | async-start | bytes 6623232 | tf_op jit(solution)/shard_map/all_gather | solution.py:76
  7.9 383.0 %reduce-scatter.2.cloned.1.call-start = ((), (), s32[]{:S(2)}) async-start(), calls=%async_computation.2 | async-start | bytes 13246464 | tf_op jit(solution)/shard_map/reduce_scatter | solution.py:103
  72.6 5.4 copy-start
  72.6 5.4 copy-start.2
  72.6 5.4 copy-start.3
  72.6 5.4 copy-start.4
  105.1 11.9 %copy-start.1 = (bf16[256,7,256]{0,2,1:T(8,128)(2,1)S(1)}, bf16[256,7,256]{0,2,1:T(8,128)(2,1)}, u32[]{:S(2)}) copy-start(bf16[256,7,256]{0,2,1:T(8,128)(2,1)} %copy.50) | copy-start | bytes 2752516 | tf_op jit(solution)/shard_map/while
  129.0 49.3 %copy-start.5 = (f32[600,256]{1,0:T(8,128)S(1)}, f32[600,256]{1,0:T(8,128)}, u32[]{:S(2)}) copy-start(f32[600,256]{1,0:T(8,128)} %get-tuple-element.332) | copy-start | bytes 1843204 | tf_op jit(solution)/shard_map/while
  178.3 353.9 %all-reduce.3.cloned.1.call-start = ((), (), s32[]{:S(2)}) async-start(), calls=%async_computation.4 | async-start | bytes 22478848
  193.0 198.0 %copy-start.6 = (u32[256]{0:T(256)S(1)}, u32[256]{0:T(256)}, u32[]{:S(2)}) copy-start(u32[256]{0:T(256)} %constant.59) | copy-start | bytes 3076
  193.0 386.2 %all-gather.6.cloned.1.call-start = ((), (), s32[]{:S(2)}) async-start(), calls=%async_computation.3 | async-start | bytes 3612672 | tf_op jit(solution)/shard_map/all_gather | solution.py:104
Sparse Core Ops, SparseCore 0:
  10.6 56.4 all-gather.3
  178.5 212.4 reduce-scatter.1
  394.4 137.7 all-reduce.2
  533.9 45.3 all-gather.5
